TPU v7x, 512 devices: a whole 4x4x16 slice. The times are simulated.
512 devices in a mesh: row: 16 (over z), col: 8 (over y, x_lo), rep: 4 (over x_hi, core).
Axes of the slice: x: 4 (x_hi: 2, x_lo: 2; x = x_hi * 2 + x_lo), y: 4, z: 16, core: 2. Of those that a mesh axis runs over, the one named last changes fastest.
Arguments:
- tokens: bfloat16 [4, 256, 16384], P('rep', 'col', 'row'), may hold values from -6 to 6
- out_grad: bfloat16 [4, 256, 8192], P('rep', 'row', 'col'), may hold values from -0.1875 to 0.1875
- moment_old: float32 [16384, 8192], P(('row', 'rep'), 'col'), may hold values from -6 to 6
- basis_old: float32 [16384, 512], P(('row', 'rep')), may hold values from -16 to 16
- factor_old: float32 [8192, 512], P('col', 'row'), may hold values from -12 to 12
- test_matrix: bfloat16 [8192, 512], P('col'), may hold values from -6 to 6
Outputs:
- moment: float32 [16384, 8192], P(('row', 'rep'), 'col')
- basis_new: float32 [16384, 512], P(('row', 'rep'))
- factor_new: float32 [8192, 512], P('col', 'row')
All inputs are finite; a program needn't handle non-finite values.
Results may differ from a plain program's by a relative error of at most 0.017.
Values may be sent and summed in bfloat16 or wider, within the bound.
A program may use at most 64 MiB of HBM per device.

v0:
```python
import functools

import jax
import jax.numpy as jnp
from jax import lax
from jax.experimental import pallas as pl
from jax.experimental.pallas import tpu as pltpu
from jax.sharding import PartitionSpec as P

MESH = pl.DeviceIdType.MESH
F32 = jnp.float32
BF16 = jnp.bfloat16
N_ROW, N_COL, N_REP = 16, 8, 4


def remote(src, dst, send, recv, device):
    return pltpu.make_async_remote_copy(
        src_ref=src, dst_ref=dst, send_sem=send, recv_sem=recv, device_id=device, device_id_type=MESH
    )


def greet(devices):
    barrier = pltpu.get_barrier_semaphore()
    for device in devices:
        pl.semaphore_signal(barrier, inc=1, device_id=device, device_id_type=MESH)
    pl.semaphore_wait(barrier, len(devices))


def others(axis, size):
    me = lax.axis_index(axis)
    return [{axis: lax.rem(me + o, size)} for o in range(1, size)]


def sketch_kernel(x_ref, out_ref, landed, send1, recv1, send2, recv2):
    me = lax.axis_index("col")
    peers = others("col", N_COL)
    greet(peers)
    rows = x_ref.shape[0] // N_COL
    first = []
    for o, peer in enumerate(peers):
        start = pl.multiple_of(peer["col"] * rows, rows)
        copy = remote(x_ref.at[pl.ds(start, rows)], landed.at[o], send1.at[o], recv1.at[o], peer)
        copy.start()
        first.append(copy)
    mine = pl.ds(pl.multiple_of(me * rows, rows), rows)
    total = x_ref[mine]
    for o in range(N_COL - 1):
        first[o].wait_recv()
        total = total + landed[o]
    out_ref[mine] = total
    second = []
    for o, peer in enumerate(peers):
        copy = remote(out_ref.at[mine], out_ref.at[mine], send2.at[o], recv2.at[o], peer)
        copy.start()
        second.append(copy)
    for copy in first:
        copy.wait_send()
    for copy in second:
        copy.wait()


def sum_sketch(x):
    rows = x.shape[0] // N_COL
    n = N_COL - 1
    return pl.pallas_call(
        sketch_kernel,
        out_shape=jax.ShapeDtypeStruct(x.shape, F32),
        in_specs=[pl.BlockSpec(memory_space=pltpu.VMEM)],
        out_specs=pl.BlockSpec(memory_space=pltpu.VMEM),
        scratch_shapes=[pltpu.VMEM((n, rows, x.shape[1]), F32)] + [pltpu.SemaphoreType.DMA((n,))] * 4,
        compiler_params=pltpu.CompilerParams(collective_id=1, has_side_effects=True, vmem_limit_bytes=32 << 20),
        name="sum_sketch",
    )(x)


def gram_kernel(x_ref, out_ref, land1, tiles, land2, s1, r1, s2, r2, s3, r3, s4, r4, s5, r5):
    row, col, rep = lax.axis_index("row"), lax.axis_index("col"), lax.axis_index("rep")
    half, core = rep // 2, lax.rem(rep, 2)
    rep_peers = others("rep", N_REP)
    row_peers = others("row", N_ROW)
    plane = []
    for h in range(2):
        for o in range(N_COL):
            if h or o:
                plane.append({"col": lax.rem(col + o, N_COL), "rep": lax.rem(half + h, 2) * 2 + core})
    sibling = {"rep": half * 2 + 1 - core}
    greet(rep_peers + row_peers + plane)

    copies = []
    for o, peer in enumerate(rep_peers):
        start = pl.multiple_of(peer["rep"] * 16, 16)
        copy = remote(x_ref.at[pl.ds(start, 16)], land1.at[o], s1.at[o], r1.at[o], peer)
        copy.start()
        copies.append(copy)
    total = x_ref[pl.ds(pl.multiple_of(rep * 16, 16), 16)]
    for o in range(N_REP - 1):
        copies[o].wait_recv()
        total = total + land1[o]
    for t in range(8):
        tiles[t] = total[8 * (t // 4) : 8 * (t // 4) + 8, 128 * (t % 4) : 128 * (t % 4) + 128]

    mine = lax.rem(row, 8)
    for o, peer in enumerate(row_peers):
        copy = remote(tiles.at[lax.rem(peer["row"], 8)], land2.at[row], s2.at[o], r2.at[o], peer)
        copy.start()
        copies.append(copy)
    land2[row] = tiles[mine]
    for o in range(N_ROW - 1):
        copies[3 + o].wait_recv()
    total = land2[0]
    for z in range(1, N_ROW):
        total = total + land2[z]
    strip = pl.multiple_of(col * 64 + rep * 16, 16)
    spot = (
        pl.ds(pl.multiple_of(strip + 8 * (mine // 4), 8), 8),
        pl.ds(pl.multiple_of(128 * lax.rem(mine, 4), 128), 128),
    )
    out_ref[spot] = total
    gather = []
    for i, o in enumerate((1, 2, 3, -1, -2, -3, -4)):
        peer = {"row": lax.rem(row + N_ROW + o, N_ROW)}
        copy = remote(out_ref.at[spot], out_ref.at[spot], s3.at[i], r3.at[i], peer)
        copy.start()
        gather.append(copy)
    for copy in gather:
        copy.wait()

    here = out_ref.at[pl.ds(strip, 16)]
    spread = []
    for i, peer in enumerate(plane):
        copy = remote(here, here, s4.at[i], r4.at[i], peer)
        copy.start()
        spread.append(copy)
    passed = remote(here, here, s5.at[15], r5.at[15], sibling)
    passed.start()
    onward = [passed]
    for h in range(2):
        for o in range(N_COL):
            if h or o:
                i = h * N_COL + o - 1
                start = lax.rem(col + N_COL - o, N_COL) * 64 + (lax.rem(half + h, 2) * 2 + core) * 16
                there = out_ref.at[pl.ds(pl.multiple_of(start, 16), 16)]
                spread[i].wait_recv()
                copy = remote(there, there, s5.at[i], r5.at[i], sibling)
                copy.start()
                onward.append(copy)
    for copy in copies + spread:
        copy.wait_send()
    for copy in onward:
        copy.wait()


def sum_gram(x):
    dma = pltpu.SemaphoreType.DMA
    sems = [dma((n,)) for n in (3, 3, 15, 15, 7, 7, 15, 15, 16, 16)]
    return pl.pallas_call(
        gram_kernel,
        out_shape=jax.ShapeDtypeStruct((x.shape[1], x.shape[1]), F32),
        in_specs=[pl.BlockSpec(memory_space=pltpu.VMEM)],
        out_specs=pl.BlockSpec(memory_space=pltpu.VMEM),
        scratch_shapes=[
            pltpu.VMEM((3, 16, 512), F32),
            pltpu.VMEM((8, 8, 128), F32),
            pltpu.VMEM((16, 8, 128), F32),
        ]
        + sems,
        compiler_params=pltpu.CompilerParams(collective_id=2, has_side_effects=True, vmem_limit_bytes=32 << 20),
        name="sum_gram",
    )(x)


def factor_kernel(x_ref, out_ref, land1, part, land2, s1, r1, s2, r2, s3, r3):
    row, rep = lax.axis_index("row"), lax.axis_index("rep")
    rep_peers = others("rep", N_REP)
    row_peers = others("row", N_ROW)
    greet(rep_peers + row_peers)
    rank, wide = x_ref.shape
    wide = wide // N_REP
    rank = rank // N_ROW
    copies = []
    for o, peer in enumerate(rep_peers):
        start = pl.multiple_of(peer["rep"] * wide, wide)
        copy = remote(x_ref.at[:, pl.ds(start, wide)], land1.at[o], s1.at[o], r1.at[o], peer)
        copy.start()
        copies.append(copy)
    mine = pl.ds(pl.multiple_of(rep * wide, wide), wide)
    for o in range(N_REP - 1):
        copies[o].wait_recv()

    def add(i, carry):
        here = pl.ds(pl.multiple_of(i * rank, rank), rank)
        total = x_ref[here, mine].astype(F32)
        for o in range(N_REP - 1):
            total = total + land1[o, here].astype(F32)
        part[i] = total.astype(BF16)
        return carry

    lax.fori_loop(0, N_ROW, add, 0)
    for o, peer in enumerate(row_peers):
        copy = remote(part.at[peer["row"]], land2.at[o], s2.at[o], r2.at[o], peer)
        copy.start()
        copies.append(copy)
    total = part[row].astype(F32)
    for o in range(N_ROW - 1):
        copies[N_REP - 1 + o].wait_recv()
        total = total + land2[o].astype(F32)
    out_ref[:, mine] = total
    for o, peer in enumerate(rep_peers):
        copy = remote(out_ref.at[:, mine], out_ref.at[:, mine], s3.at[o], r3.at[o], peer)
        copy.start()
        copy_out = copy
        copies.append(copy_out)
    for copy in copies[N_REP - 1 + N_ROW - 1 :]:
        copy.wait_recv()
    for copy in copies:
        copy.wait_send()


def sum_factor(x):
    dma = pltpu.SemaphoreType.DMA
    rank, wide = x.shape[0] // N_ROW, x.shape[1] // N_REP
    return pl.pallas_call(
        factor_kernel,
        out_shape=jax.ShapeDtypeStruct((rank, x.shape[1]), F32),
        in_specs=[pl.BlockSpec(memory_space=pltpu.VMEM)],
        out_specs=pl.BlockSpec(memory_space=pltpu.VMEM),
        scratch_shapes=[
            pltpu.VMEM((N_REP - 1, x.shape[0], wide), BF16),
            pltpu.VMEM((N_ROW, rank, wide), BF16),
            pltpu.VMEM((N_ROW - 1, rank, wide), BF16),
        ]
        + [dma((n,)) for n in (3, 3, 15, 15, 3, 3)],
        compiler_params=pltpu.CompilerParams(collective_id=3, has_side_effects=True, vmem_limit_bytes=32 << 20),
        name="sum_factor",
    )(x)


def gather_kernel(tok_ref, og_ref, fa_ref, tk_ref, g_ref, f_ref, rs, rr, ss, sr, xs, xr, ts, tr, cs, cr):
    row, col, rep = lax.axis_index("row"), lax.axis_index("col"), lax.axis_index("rep")
    half, core = rep // 2, lax.rem(rep, 2)
    across = (1 - half) * 2 + core
    sibling = half * 2 + 1 - core
    rep_peers = others("rep", N_REP)
    col_peers = others("col", N_COL)
    sides = ({"row": lax.rem(row + 1, N_ROW)}, {"row": lax.rem(row + N_ROW - 1, N_ROW)})
    wide = tok_ref.shape[1] // N_REP
    part = pl.ds(pl.multiple_of(rep * wide, wide), wide)
    g_ref[rep, row] = og_ref[...]
    f_ref[row, 0] = fa_ref[:16]
    f_ref[row, 1] = fa_ref[16:]
    tk_ref[col, rep] = tok_ref[:, part]
    greet(rep_peers + col_peers + list(sides))

    def slot(stream, z, c=core):
        if stream == 2:
            return f_ref.at[z, c]
        return g_ref.at[(half if stream == 0 else 1 - half) * 2 + c, z]

    def ring(stream, side, step):
        z = lax.rem(row + N_ROW + (1 - step if side == 0 else step - 1), N_ROW)
        return remote(slot(stream, z), slot(stream, z), rs.at[stream, side, step], rr.at[stream, side, step], sides[side])

    def arrival(stream, side, step):
        z = lax.rem(row + N_ROW + (-step if side == 0 else step), N_ROW)
        return remote(slot(stream, z), slot(stream, z), rs.at[stream, side, step], rr.at[stream, side, step], sides[side])

    def hand(stream, index, c=core):
        z = lax.rem(row + N_ROW + jnp.where(index <= 8, -index, index - 8), N_ROW)
        return remote(slot(stream, z, c), slot(stream, z, c), ss.at[stream, index], sr.at[stream, index], {"rep": sibling})

    swap = remote(slot(0, row), slot(0, row), xs, xr, {"rep": across})
    swap.start()
    for stream in (0, 2):
        for side in range(2):
            ring(stream, side, 1).start()
    first = []
    for o, peer in enumerate(rep_peers):
        start = pl.multiple_of(peer["rep"] * wide, wide)
        copy = remote(tok_ref.at[:, pl.ds(start, wide)], tk_ref.at[col, rep], ts.at[o], tr.at[o], peer)
        copy.start()
        first.append(copy)
    hand(0, 0).start()
    swap.wait_recv()
    for side in range(2):
        ring(1, side, 1).start()
    hand(1, 0).start()
    for copy in first:
        copy.wait_recv()
    second = []
    for o, peer in enumerate(col_peers):
        copy = remote(tk_ref.at[col], tk_ref.at[col], cs.at[o], cr.at[o], peer)
        copy.start()
        second.append(copy)

    def step(s, carry):
        for stream in (0, 2, 1):
            arrival(stream, 0, s).wait_recv()
            ring(stream, 0, s + 1).start()
            hand(stream, s).start()
            arrival(stream, 1, s).wait_recv()

            @pl.when(s < 7)
            def _():
                ring(stream, 1, s + 1).start()

            hand(stream, s + 8).start()
        return carry

    lax.fori_loop(1, 8, step, 0)
    for stream in (0, 2, 1):
        arrival(stream, 0, 8).wait_recv()
        hand(stream, 8).start()
    for copy in second:
        copy.wait_recv()

    def finish(i, carry):
        for stream in range(3):
            hand(stream, i, 1 - core).wait_recv()
            hand(stream, i).wait_send()
        return carry

    for stream in range(2):
        hand(stream, 0, 1 - core).wait_recv()
        hand(stream, 0).wait_send()
    lax.fori_loop(1, 16, finish, 0)

    def drain(s, carry):
        for stream in range(3):
            for side in range(2):
                ring(stream, side, s).wait_send()
        return carry

    lax.fori_loop(1, 8, drain, 0)
    for stream in range(3):
        ring(stream, 0, 8).wait_send()
    swap.wait_send()
    for copy in first + second:
        copy.wait_send()


def gather(tokens, out_grad, factor):
    dma = pltpu.SemaphoreType.DMA
    vmem = pl.BlockSpec(memory_space=pltpu.VMEM)
    depth, wide = tokens.shape[0], tokens.shape[1] // N_REP
    tall, across = out_grad.shape
    return pl.pallas_call(
        gather_kernel,
        out_shape=(
            jax.ShapeDtypeStruct((N_COL, N_REP, depth, wide), BF16),
            jax.ShapeDtypeStruct((N_REP, N_ROW, tall, across), BF16),
            jax.ShapeDtypeStruct((N_ROW, 2, factor.shape[0] // 2, across), BF16),
        ),
        in_specs=[vmem] * 3,
        out_specs=(vmem,) * 3,
        scratch_shapes=[
            dma((3, 2, 9)), dma((3, 2, 9)), dma((3, 16)), dma((3, 16)), dma, dma,
            dma((3,)), dma((3,)), dma((7,)), dma((7,)),
        ],
        compiler_params=pltpu.CompilerParams(collective_id=4, has_side_effects=True, vmem_limit_bytes=32 << 20),
        name="gather",
    )(tokens, out_grad, factor)


def tile_kernel(tk_ref, g_ref, f_ref, moment_ref, basis_ref, test_ref, new_ref, second_ref, part_ref, high, low):
    step = 256
    high[...] = basis_ref[...].astype(BF16)
    low[...] = (basis_ref[...] - high[...].astype(F32)).astype(BF16)
    rank = basis_ref.shape[1]
    part_ref[...] = jnp.zeros_like(part_ref)

    def columns(i, carry):
        here = pl.ds(pl.multiple_of(i * step, step), step)
        gradient = jnp.zeros((new_ref.shape[0], step), F32)
        for b in range(N_REP):
            left = tk_ref[:, b].reshape(-1, tk_ref.shape[3])
            right = g_ref[b, :, :, here].reshape(-1, step)
            piece = lax.dot_general(left, right, (((0,), (0,)), ((), ())), preferred_element_type=F32)
            gradient = gradient + piece.astype(BF16).astype(F32)
        new_ref[:, here] = 0.9 * moment_ref[:, here] + 0.1 * gradient
        factor = f_ref[:, :, :, here].reshape(rank, step)
        previous = jnp.dot(high[...], factor, preferred_element_type=F32)
        previous = previous + jnp.dot(low[...], factor, preferred_element_type=F32)
        second = (0.95 * previous + 0.05 * gradient * gradient).astype(BF16)
        second_ref[:, here] = second
        part_ref[...] += jnp.dot(second, test_ref[here], preferred_element_type=F32)
        return carry

    lax.fori_loop(0, new_ref.shape[1] // step, columns, 0)


def tile(tk, g, f, moment_old, basis_old, test_matrix):
    vmem = pl.BlockSpec(memory_space=pltpu.VMEM)
    rows, columns = moment_old.shape
    rank = basis_old.shape[1]
    return pl.pallas_call(
        tile_kernel,
        out_shape=(
            jax.ShapeDtypeStruct((rows, columns), F32),
            jax.ShapeDtypeStruct((rows, columns), BF16),
            jax.ShapeDtypeStruct((rows, rank), F32),
        ),
        in_specs=[vmem] * 6,
        out_specs=(vmem,) * 3,
        scratch_shapes=[pltpu.VMEM((rows, rank), BF16)] * 2,
        compiler_params=pltpu.CompilerParams(vmem_limit_bytes=32 << 20),
        name="tile",
    )(tk, g, f, moment_old, basis_old, test_matrix)


SPAN = 128


def invert_diagonal(block):
    count = SPAN // 8
    d = [block[8 * i : 8 * i + 8, :] for i in range(count)]
    lane = lax.broadcasted_iota(jnp.int32, (8, SPAN), 1)
    sub = lax.broadcasted_iota(jnp.int32, (8, SPAN), 0)
    x = [jnp.where(lane == sub + 8 * i, 1.0, 0.0).astype(F32) for i in range(count)]
    out = []

    def spread(value):
        return jnp.broadcast_to(value, (8, SPAN))

    for b0 in range(count):
        j0 = 8 * b0
        rows, extra = d[b0], x[b0]
        wide = [spread(rows[:, j0 + m : j0 + m + 1]) for m in range(8)]
        s = [[spread(wide[m][i : i + 1, :]) if m <= i else None for m in range(8)] for i in range(8)]
        p = [spread(rows[i : i + 1, :]) for i in range(8)]
        q = [spread(extra[i : i + 1, :]) for i in range(8)]
        inverse = [None] * 8
        f = [[None] * 8 for _ in range(8)]
        for m in range(8):
            inverse[m] = 1.0 / s[m][m]
            for i in range(m + 1, 8):
                f[i][m] = s[i][m] * inverse[m]
            for i in range(m + 1, 8):
                for l in range(m + 1, i + 1):
                    s[i][l] = s[i][l] - f[i][m] * s[l][m]
            for i in range(m + 1, 8):
                p[i] = p[i] - f[i][m] * p[m]
                q[i] = q[i] - f[i][m] * q[m]
        done = jnp.zeros((8, SPAN), F32)
        for i in range(8):
            done = jnp.where(sub == i, q[i] * lax.rsqrt(s[i][i]), done)
        out.append(done)
        v, w = [None] * 8, [None] * 8
        for i in reversed(range(8)):
            v[i] = p[i] * inverse[i]
            w[i] = q[i] * inverse[i]
            for m in range(i + 1, 8):
                v[i] = v[i] - f[m][i] * v[m]
                w[i] = w[i] - f[m][i] * w[m]
        for b in range(b0 + 1, count):
            source, left, right = d[b], d[b], x[b]
            for m in range(8):
                c = spread(source[:, j0 + m : j0 + m + 1])
                left = left - c * v[m]
                right = right - c * w[m]
            d[b], x[b] = left, right
    return jnp.concatenate(out, 0)


def exact(a, b, dims):
    return lax.dot_general(a, b, (dims, ((), ())), precision=lax.Precision.HIGHEST, preferred_element_type=F32)


def inverse_kernel(g_ref, m_ref, a):
    n = g_ref.shape[0]
    eye = lax.broadcasted_iota(jnp.int32, (n, n), 0) == lax.broadcasted_iota(jnp.int32, (n, n), 1)
    gram = g_ref[...]
    shift = 0.01 * jnp.sum(jnp.where(eye, gram, 0.0)) / n
    a[...] = jnp.where(eye, gram + shift, gram)
    m_ref[...] = jnp.where(eye, 1.0, 0.0).astype(F32)
    for k in range(n // SPAN):
        end = (k + 1) * SPAN
        own, rest = slice(k * SPAN, end), slice(end, n)
        inverse = invert_diagonal(a[own, own])
        rows = exact(inverse, m_ref[own, :end], ((1,), (0,)))
        m_ref[own, :end] = rows
        if end < n:
            panel = exact(a[rest, own], inverse, ((1,), (1,)))
            a[rest, rest] = a[rest, rest] - exact(panel, panel, ((1,), (1,)))
            m_ref[rest, :end] = m_ref[rest, :end] - exact(panel, rows, ((1,), (0,)))


def inverse_factor(gram):
    vmem = pl.BlockSpec(memory_space=pltpu.VMEM)
    return pl.pallas_call(
        inverse_kernel,
        out_shape=jax.ShapeDtypeStruct(gram.shape, F32),
        in_specs=[vmem],
        out_specs=vmem,
        scratch_shapes=[pltpu.VMEM(gram.shape, F32)],
        compiler_params=pltpu.CompilerParams(vmem_limit_bytes=32 << 20),
        name="inverse_factor",
    )(gram)


def shards(tokens, out_grad, moment_old, basis_old, factor_old, test_matrix):
    tk, g, f = gather(tokens[0], out_grad[0], factor_old.T.astype(BF16))
    moment, second, part = tile(tk, g, f, moment_old, basis_old, test_matrix)
    sketch = sum_sketch(part)
    block = sketch.shape[1] // N_COL
    own = lax.dynamic_slice_in_dim(sketch, lax.axis_index("col") * block, block, 1)
    gram_matrix = sum_gram(jnp.dot(own.T, sketch, precision=lax.Precision.HIGHEST))
    inverse = inverse_factor(gram_matrix)
    orthonormal = jnp.dot(sketch, inverse.T, precision=lax.Precision.HIGHEST)
    basis_bf = orthonormal.astype(jnp.bfloat16)
    product = lax.dot_general(
        basis_bf, second, (((0,), (0,)), ((), ())), preferred_element_type=jnp.float32
    )
    factor_new = sum_factor(product.astype(BF16)).T
    return (moment, orthonormal, factor_new)


def solution(mesh):
    placed = (
        P("rep", "col", "row"),
        P("rep", "row", "col"),
        P(("row", "rep"), "col"),
        P(("row", "rep"), None),
        P("col", "row"),
        P("col", None),
    )
    return jax.shard_map(
        shards,
        mesh=mesh,
        in_specs=placed,
        out_specs=(P(("row", "rep"), "col"), P(("row", "rep"), None), P("col", "row")),
        check_vma=False,
    )
```

profile of v0, /device:TPU:1, one launch (start us, length us, event | category | flops | bytes accessed | tf_op | source)
XLA Modules:
  0.0 176.5 jit_solution(6693538901040463521)
XLA Ops:
  0.6 0.9 convert_bitcast_fusion.fa_ref
  1.5 0.0 copy-start.3
  1.6 0.8 copy-done.3
  2.4 0.0 copy-start.4
  2.4 0.8 copy-done.4
  3.1 47.8 %gather.1 = (bf16[8,4,32,256]{3,2,1,0:T(8,128)(2,1)S(1)}, bf16[4,16,16,1024]{3,2,1,0:T(8,128)(2,1)S(1)}, bf16[16,2,16,1024]{3,2,1,0:T(8,128)(2,1)S(1)}) custom-call(bf16[32,1024]{1,0:T(8,128)(2,1)S(1)} %bitcast.10, bf16[16,1024]{1,0:T(8,128)(2,1)S(1)} %bitcast.11, bf16[32,1024]{1,0:T(8,128)(2,1)S(1)} %convert_bitcast_fusion.fa_ref), custom_call_target="tpu_custom_call" | custom-call | tf_op jit(solution)/shard_map/gather/pallas_call | solution.py:346
  50.9 0.0 copy-start
  50.9 1.2 copy-done
  52.1 0.0 copy-start.1
  52.1 1.2 copy-done.1
  53.4 0.0 copy-start.2
  53.4 1.0 copy-done.2
  54.4 3.7 %tile.1 = (f32[256,1024]{1,0:T(8,128)}, bf16[256,1024]{1,0:T(8,128)(2,1)S(1)}, f32[256,512]{1,0:T(8,128)S(1)}) custom-call(bf16[8,4,32,256]{3,2,1,0:T(8,128)(2,1)S(1)} %get-tuple-element.9.tk_ref, bf16[4,16,16,1024]{3,2,1,0:T(8,128)(2,1)S(1)} %get-tuple-element.10.g_ref, bf16[16,2,16,1024]{3,2,1,0:T(8,128)(2,1)S(1)} %get-tuple-element.11.f_ref, ...), custom_call_target="tpu_custom_call" | custom-call | tf_op jit(solution)/shard_map/tile/pallas_call | solution.py:395
  58.1 17.4 %sum_sketch.1 = f32[256,512]{1,0:T(8,128)S(1)} custom-call(f32[256,512]{1,0:T(8,128)S(1)} %get-tuple-element.13.x_ref), custom_call_target="tpu_custom_call" | custom-call | tf_op jit(solution)/shard_map/sum_sketch/pallas_call | solution.py:65
  75.5 0.4 fusion.1.x_ref
  76.0 33.3 %sum_gram.1.g_ref = f32[512,512]{1,0:T(8,128)S(1)} custom-call(f32[64,512]{1,0:T(8,128)S(1)} %fusion.1.x_ref), custom_call_target="tpu_custom_call" | custom-call | tf_op jit(solution)/shard_map/sum_gram/pallas_call | solution.py:156
  109.3 28.9 %inverse_factor.1 = f32[512,512]{1,0:T(8,128)S(1)} custom-call(f32[512,512]{1,0:T(8,128)S(1)} %sum_gram.1.g_ref), custom_call_target="tpu_custom_call" | custom-call | tf_op jit(solution)/shard_map/inverse_factor/pallas_call | solution.py:489
  138.2 1.1 fusion.4
  139.3 0.0 copy-start.5
  139.3 0.5 convolution_convert_fusion.x_ref
  139.7 36.1 %sum_factor.1 = f32[32,1024]{1,0:T(8,128)S(1)} custom-call(bf16[512,1024]{1,0:T(8,128)(2,1)S(1)} %convolution_convert_fusion.x_ref), custom_call_target="tpu_custom_call" | custom-call | tf_op jit(solution)/shard_map/sum_factor/pallas_call | solution.py:222
  175.8 0.7 copy.10
  176.5 0.0 copy-done.5
Async XLA Ops:
  1.5 0.8 copy-start.3
  2.4 0.8 copy-start.4
  50.9 1.2 copy-start
  52.1 1.2 copy-start.1
  53.4 1.0 copy-start.2
  139.3 37.2 %copy-start.5 = (f32[256,512]{1,0:T(8,128)}, f32[256,512]{1,0:T(8,128)S(1)}, u32[]{:S(2)}) copy-start(f32[256,512]{1,0:T(8,128)S(1)} %fusion.4) | copy-start | bytes 1572868
where the time goes:
time: 177 us; the launch traced here: 176 us
  Pallas kernels  167 us (94%)
  local copies, waits for them, and re-layouts  5.74 us (3%)
  matrix products  1.96 us (1%)
    pallas_call x1, Pallas kernels, gather(): pl.pallas_call(gather_kernel, out_shape=(jax.ShapeDtypeStruct((N_COL, N_R...  47.8 us
    pallas_call x1, Pallas kernels, sum_factor(): pl.pallas_call(factor_kernel, out_shape=jax.ShapeDtypeStruct((rank, x.sha...  36.1 us
    pallas_call x1, Pallas kernels, sum_gram(): pl.pallas_call(gram_kernel, out_shape=jax.ShapeDtypeStruct((x.shape[1], x...  33.3 us
    pallas_call x1, Pallas kernels, inverse_factor(): pl.pallas_call(inverse_kernel, out_shape=jax.ShapeDtypeStruct(gram.shape,...  28.9 us
    pallas_call x1, Pallas kernels, sum_sketch(): pl.pallas_call(sketch_kernel, out_shape=jax.ShapeDtypeStruct(x.shape, F32...  17.4 us
    unnamed x13, local copies, waits for them, and re-layouts  5.74 us
    pallas_call x1, Pallas kernels, tile(): pl.pallas_call(tile_kernel, out_shape=(jax.ShapeDtypeStruct((rows, column...  3.74 us

commit v1 on v0

v1 whole, which is shorter than its diff:
```python
import functools

import jax
import jax.numpy as jnp
from jax import lax
from jax.experimental import pallas as pl
from jax.experimental.pallas import tpu as pltpu
from jax.sharding import PartitionSpec as P

MESH = pl.DeviceIdType.MESH
F32 = jnp.float32
BF16 = jnp.bfloat16
N_ROW, N_COL, N_REP = 16, 8, 4


def remote(src, dst, send, recv, device):
    return pltpu.make_async_remote_copy(
        src_ref=src, dst_ref=dst, send_sem=send, recv_sem=recv, device_id=device, device_id_type=MESH
    )


def greet(devices):
    barrier = pltpu.get_barrier_semaphore()
    for device in devices:
        pl.semaphore_signal(barrier, inc=1, device_id=device, device_id_type=MESH)
    pl.semaphore_wait(barrier, len(devices))


def others(axis, size):
    me = lax.axis_index(axis)
    return [{axis: lax.rem(me + o, size)} for o in range(1, size)]


def gather_kernel(tok_ref, og_ref, fa_ref, tk_ref, g_ref, f_ref, rs, rr, ss, sr, xs, xr, ts, tr, cs, cr):
    row, col, rep = lax.axis_index("row"), lax.axis_index("col"), lax.axis_index("rep")
    half, core = rep // 2, lax.rem(rep, 2)
    across = (1 - half) * 2 + core
    sibling = half * 2 + 1 - core
    rep_peers = others("rep", N_REP)
    col_peers = others("col", N_COL)
    sides = ({"row": lax.rem(row + 1, N_ROW)}, {"row": lax.rem(row + N_ROW - 1, N_ROW)})
    wide = tok_ref.shape[1] // N_REP
    part = pl.ds(pl.multiple_of(rep * wide, wide), wide)
    g_ref[rep, row] = og_ref[...]
    f_ref[row, 0] = fa_ref[:16]
    f_ref[row, 1] = fa_ref[16:]
    tk_ref[col, rep] = tok_ref[:, part]
    greet(rep_peers + col_peers + list(sides))

    def slot(stream, z, c=core):
        if stream == 2:
            return f_ref.at[z, c]
        return g_ref.at[(half if stream == 0 else 1 - half) * 2 + c, z]

    def ring(stream, side, step):
        z = lax.rem(row + N_ROW + (1 - step if side == 0 else step - 1), N_ROW)
        return remote(slot(stream, z), slot(stream, z), rs.at[stream, side, step], rr.at[stream, side, step], sides[side])

    def arrival(stream, side, step):
        z = lax.rem(row + N_ROW + (-step if side == 0 else step), N_ROW)
        return remote(slot(stream, z), slot(stream, z), rs.at[stream, side, step], rr.at[stream, side, step], sides[side])

    def hand(stream, index, c=core):
        z = lax.rem(row + N_ROW + jnp.where(index <= 8, -index, index - 8), N_ROW)
        return remote(slot(stream, z, c), slot(stream, z, c), ss.at[stream, index], sr.at[stream, index], {"rep": sibling})

    swap = remote(slot(0, row), slot(0, row), xs, xr, {"rep": across})
    swap.start()
    for stream in (0, 2):
        for side in range(2):
            ring(stream, side, 1).start()
    first = []
    for o, peer in enumerate(rep_peers):
        start = pl.multiple_of(peer["rep"] * wide, wide)
        copy = remote(tok_ref.at[:, pl.ds(start, wide)], tk_ref.at[col, rep], ts.at[o], tr.at[o], peer)
        copy.start()
        first.append(copy)
    hand(0, 0).start()
    swap.wait_recv()
    for side in range(2):
        ring(1, side, 1).start()
    hand(1, 0).start()
    for copy in first:
        copy.wait_recv()
    second = []
    for o, peer in enumerate(col_peers):
        copy = remote(tk_ref.at[col], tk_ref.at[col], cs.at[o], cr.at[o], peer)
        copy.start()
        second.append(copy)

    def step(s, carry):
        for stream in (0, 2, 1):
            arrival(stream, 0, s).wait_recv()
            ring(stream, 0, s + 1).start()
            hand(stream, s).start()
            arrival(stream, 1, s).wait_recv()

            @pl.when(s < 7)
            def _():
                ring(stream, 1, s + 1).start()

            hand(stream, s + 8).start()
        return carry

    lax.fori_loop(1, 8, step, 0)
    for stream in (0, 2, 1):
        arrival(stream, 0, 8).wait_recv()
        hand(stream, 8).start()
    for copy in second:
        copy.wait_recv()

    def finish(i, carry):
        for stream in range(3):
            hand(stream, i, 1 - core).wait_recv()
            hand(stream, i).wait_send()
        return carry

    for stream in range(2):
        hand(stream, 0, 1 - core).wait_recv()
        hand(stream, 0).wait_send()
    lax.fori_loop(1, 16, finish, 0)

    def drain(s, carry):
        for stream in range(3):
            for side in range(2):
                ring(stream, side, s).wait_send()
        return carry

    lax.fori_loop(1, 8, drain, 0)
    for stream in range(3):
        ring(stream, 0, 8).wait_send()
    swap.wait_send()
    for copy in first + second:
        copy.wait_send()


def gather(tokens, out_grad, factor):
    dma = pltpu.SemaphoreType.DMA
    vmem = pl.BlockSpec(memory_space=pltpu.VMEM)
    depth, wide = tokens.shape[0], tokens.shape[1] // N_REP
    tall, across = out_grad.shape
    return pl.pallas_call(
        gather_kernel,
        out_shape=(
            jax.ShapeDtypeStruct((N_COL, N_REP, depth, wide), BF16),
            jax.ShapeDtypeStruct((N_REP, N_ROW, tall, across), BF16),
            jax.ShapeDtypeStruct((N_ROW, 2, factor.shape[0] // 2, across), BF16),
        ),
        in_specs=[vmem] * 3,
        out_specs=(vmem,) * 3,
        scratch_shapes=[
            dma((3, 2, 9)), dma((3, 2, 9)), dma((3, 16)), dma((3, 16)), dma, dma,
            dma((3,)), dma((3,)), dma((7,)), dma((7,)),
        ],
        compiler_params=pltpu.CompilerParams(collective_id=4, has_side_effects=True, vmem_limit_bytes=12 << 20),
        name="gather",
    )(tokens, out_grad, factor)


def tile_kernel(tk_ref, g_ref, f_ref, moment_ref, basis_ref, test_ref, new_ref, second_ref, part_ref, high, low):
    step = 256
    high[...] = basis_ref[...].astype(BF16)
    low[...] = (basis_ref[...] - high[...].astype(F32)).astype(BF16)
    rank = basis_ref.shape[1]
    part_ref[...] = jnp.zeros_like(part_ref)

    def columns(i, carry):
        here = pl.ds(pl.multiple_of(i * step, step), step)
        gradient = jnp.zeros((new_ref.shape[0], step), F32)
        for b in range(N_REP):
            left = tk_ref[:, b].reshape(-1, tk_ref.shape[3])
            right = g_ref[b, :, :, here].reshape(-1, step)
            piece = lax.dot_general(left, right, (((0,), (0,)), ((), ())), preferred_element_type=F32)
            gradient = gradient + piece.astype(BF16).astype(F32)
        new_ref[:, here] = 0.9 * moment_ref[:, here] + 0.1 * gradient
        factor = f_ref[:, :, :, here].reshape(rank, step)
        previous = jnp.dot(high[...], factor, preferred_element_type=F32)
        previous = previous + jnp.dot(low[...], factor, preferred_element_type=F32)
        second = (0.95 * previous + 0.05 * gradient * gradient).astype(BF16)
        second_ref[:, here] = second
        part_ref[...] += jnp.dot(second, test_ref[here], preferred_element_type=F32)
        return carry

    lax.fori_loop(0, new_ref.shape[1] // step, columns, 0)


def tile(tk, g, f, moment_old, basis_old, test_matrix):
    vmem = pl.BlockSpec(memory_space=pltpu.VMEM)
    rows, columns = moment_old.shape
    rank = basis_old.shape[1]
    return pl.pallas_call(
        tile_kernel,
        out_shape=(
            jax.ShapeDtypeStruct((rows, columns), F32),
            jax.ShapeDtypeStruct((rows, columns), BF16),
            jax.ShapeDtypeStruct((rows, rank), F32),
        ),
        in_specs=[vmem] * 6,
        out_specs=(vmem,) * 3,
        scratch_shapes=[pltpu.VMEM((rows, rank), BF16)] * 2,
        compiler_params=pltpu.CompilerParams(vmem_limit_bytes=20 << 20),
        name="tile",
    )(tk, g, f, moment_old, basis_old, test_matrix)


SPAN = 128


def invert_diagonal(block):
    sub = lax.broadcasted_iota(jnp.int32, (8, SPAN), 0)
    shape = (SPAN, SPAN)
    d = block
    x = (lax.broadcasted_iota(jnp.int32, shape, 0) == lax.broadcasted_iota(jnp.int32, shape, 1)).astype(F32)
    out = []

    def spread(value):
        return jnp.broadcast_to(value, (8, SPAN))

    for j0 in range(0, SPAN, 8):
        wide = [spread(d[:8, j0 + m : j0 + m + 1]) for m in range(8)]
        s = [[spread(wide[m][i : i + 1, :]) if m <= i else None for m in range(8)] for i in range(8)]
        p = [spread(d[i : i + 1, :]) for i in range(8)]
        q = [spread(x[i : i + 1, :]) for i in range(8)]
        inverse = [None] * 8
        f = [[None] * 8 for _ in range(8)]
        for m in range(8):
            inverse[m] = 1.0 / s[m][m]
            for i in range(m + 1, 8):
                f[i][m] = s[i][m] * inverse[m]
            for i in range(m + 1, 8):
                for l in range(m + 1, i + 1):
                    s[i][l] = s[i][l] - f[i][m] * s[l][m]
            for i in range(m + 1, 8):
                p[i] = p[i] - f[i][m] * p[m]
                q[i] = q[i] - f[i][m] * q[m]
        done = q[0] * lax.rsqrt(s[0][0])
        for i in range(1, 8):
            done = jnp.where(sub == i, q[i] * lax.rsqrt(s[i][i]), done)
        out.append(done)
        if j0 + 8 == SPAN:
            break
        v, w = [None] * 8, [None] * 8
        for i in reversed(range(8)):
            v[i] = p[i] * inverse[i]
            w[i] = q[i] * inverse[i]
            for m in range(i + 1, 8):
                v[i] = v[i] - f[m][i] * v[m]
                w[i] = w[i] - f[m][i] * w[m]
        d, x = d[8:], x[8:]
        source = d
        for m in range(8):
            c = source[:, j0 + m : j0 + m + 1]
            d = d - c * v[m][:1]
            x = x - c * w[m][:1]
    return jnp.concatenate(out, 0)


def exact(a, b, dims):
    return lax.dot_general(a, b, (dims, ((), ())), precision=lax.Precision.HIGHEST, preferred_element_type=F32)


def range_kernel(
    part_ref, second_ref, basis_ref, fac_ref,
    send_sk, land_sk, sk, gram, out, land1, tiles, land2, z, land_c, land_x, land_z, z_all, packed, m_ref, a_ref,
    s1, r1, s2, r2, s3, r3, s4, r4, s5, r5, s6, r6, s7, r7, zs1, zr1, zs2, zr2, zs3, zr3, zs4, zr4, fs, fr,
):
    row, col, rep = lax.axis_index("row"), lax.axis_index("col"), lax.axis_index("rep")
    half, core = rep // 2, lax.rem(rep, 2)
    rep_peers = others("rep", N_REP)
    row_peers = others("row", N_ROW)
    col_peers = others("col", N_COL)
    sibling = {"rep": half * 2 + 1 - core}
    across = {"rep": (1 - half) * 2 + core}
    plane = []
    for h in range(2):
        for o in range(N_COL):
            if h or o:
                plane.append({"col": lax.rem(col + o, N_COL), "rep": lax.rem(half + h, 2) * 2 + core})
    sends = []

    def start(src, dst, send, recv, device):
        copy = remote(src, dst, send, recv, device)
        copy.start()
        sends.append(copy)
        return copy

    send_sk[...] = part_ref[...].astype(BF16)
    greet(rep_peers + row_peers + plane)
    rows = part_ref.shape[0] // N_COL
    mine = pl.ds(pl.multiple_of(col * rows, rows), rows)
    copies = []
    for o, peer in enumerate(col_peers):
        there = pl.ds(pl.multiple_of(peer["col"] * rows, rows), rows)
        copies.append(start(send_sk.at[there], land_sk.at[o], s1.at[o], r1.at[o], peer))
    total = part_ref[mine]
    for o in range(N_COL - 1):
        copies[o].wait_recv()
        total = total + land_sk[o].astype(F32)
    sk[mine] = total.astype(BF16)
    copies = [start(sk.at[mine], sk.at[mine], s2.at[o], r2.at[o], peer) for o, peer in enumerate(col_peers)]
    for copy in copies:
        copy.wait_recv()

    sketch = sk[...]
    gram[...] = lax.dot_general(sketch, sketch, (((0,), (0,)), ((), ())), preferred_element_type=F32)
    copies = []
    for o, peer in enumerate(rep_peers):
        there = pl.ds(pl.multiple_of(col * 64 + peer["rep"] * 16, 16), 16)
        copies.append(start(gram.at[there], land1.at[o], s3.at[o], r3.at[o], peer))

    for i in range(4):
        piece = lax.dot_general(
            second_ref[:, 256 * i : 256 * i + 256], sketch, (((0,), (0,)), ((), ())), preferred_element_type=F32
        )
        z[4 * i : 4 * i + 4] = piece.reshape(4, N_REP, 16, sketch.shape[1])

    strip = pl.multiple_of(col * 64 + rep * 16, 16)
    total = gram[pl.ds(strip, 16)]
    for o in range(N_REP - 1):
        copies[o].wait_recv()
        total = total + land1[o]
    for t in range(8):
        tiles[t] = total[8 * (t // 4) : 8 * (t // 4) + 8, 128 * (t % 4) : 128 * (t % 4) + 128]
    tile_no = lax.rem(row, 8)
    copies = []
    for o, peer in enumerate(row_peers):
        copies.append(start(tiles.at[lax.rem(peer["row"], 8)], land2.at[row], s4.at[o], r4.at[o], peer))
    land2[row] = tiles[tile_no]

    z_core = [
        start(z.at[:, 2 * h + 1 - core], land_c.at[h], zs1.at[h], zr1.at[h], sibling) for h in range(2)
    ]

    for o in range(N_ROW - 1):
        copies[o].wait_recv()
    total = land2[0]
    for i in range(1, N_ROW):
        total = total + land2[i]
    spot = (
        pl.ds(pl.multiple_of(strip + 8 * (tile_no // 4), 8), 8),
        pl.ds(pl.multiple_of(128 * lax.rem(tile_no, 4), 128), 128),
    )
    out[spot] = total
    copies = []
    for i, o in enumerate((1, 2, 3, -1, -2, -3, -4)):
        peer = {"row": lax.rem(row + N_ROW + o, N_ROW)}
        copies.append(start(out.at[spot], out.at[spot], s5.at[i], r5.at[i], peer))

    for copy in z_core:
        copy.wait_recv()

    def add_core(i, carry):
        for h in range(2):
            land_c[h, i] = land_c[h, i] + z[i, 2 * h + core]
        return carry

    lax.fori_loop(0, N_ROW, add_core, 0)

    for copy in copies:
        copy.wait_recv()
    here = out.at[pl.ds(strip, 16)]
    copies = [start(here, here, s6.at[i], r6.at[i], peer) for i, peer in enumerate(plane)]
    onward = [start(here, here, s7.at[15], r7.at[15], sibling)]
    z_across = start(land_c.at[1 - half], land_x, zs2, zr2, across)
    for h in range(2):
        for o in range(N_COL):
            if h or o:
                i = h * N_COL + o - 1
                first = lax.rem(col + N_COL - o, N_COL) * 64 + (lax.rem(half + h, 2) * 2 + core) * 16
                there = out.at[pl.ds(pl.multiple_of(first, 16), 16)]
                copies[i].wait_recv()
                onward.append(start(there, there, s7.at[i], r7.at[i], sibling))

    z_across.wait_recv()

    def add_across(i, carry):
        land_x[i] = land_x[i] + land_c[half, i]
        return carry

    lax.fori_loop(0, N_ROW, add_across, 0)
    z_row = [
        start(land_x.at[peer["row"]], land_z.at[o], zs3.at[o], zr3.at[o], peer) for o, peer in enumerate(row_peers)
    ]
    for copy in onward:
        copy.wait_recv()

    n = gram.shape[0]
    eye = lax.broadcasted_iota(jnp.int32, (n, n), 0) == lax.broadcasted_iota(jnp.int32, (n, n), 1)
    whole = out[...]
    shift = 0.01 * jnp.sum(jnp.where(eye, whole, 0.0)) / n
    a_ref[...] = jnp.where(eye, whole + shift, whole)
    m_ref[...] = jnp.where(eye, 1.0, 0.0).astype(F32)
    z_rep = []
    for k in range(n // SPAN):
        end = (k + 1) * SPAN
        own, rest = slice(k * SPAN, end), slice(end, n)
        if end == n:
            z_sum = land_x[row]
            for o in range(N_ROW - 1):
                z_row[o].wait_recv()
                z_sum = z_sum + land_z[o]
            z_all[rep] = z_sum
            for o, peer in enumerate(rep_peers):
                z_rep.append(start(z_all.at[rep], z_all.at[rep], zs4.at[o], zr4.at[o], peer))
        inverse = invert_diagonal(a_ref[own, own])
        block = exact(inverse, m_ref[own, :end], ((1,), (0,)))
        m_ref[own, :end] = block
        if end < n:
            panel = exact(a_ref[rest, own], inverse, ((1,), (1,)))
            a_ref[rest, rest] = a_ref[rest, rest] - exact(panel, panel, ((1,), (1,)))
            m_ref[rest, :end] = m_ref[rest, :end] - exact(panel, block, ((1,), (0,)))

    for copy in z_rep:
        copy.wait_recv()
    new = exact(z_all[...].reshape(N_REP * 16, n), m_ref[...], ((1,), (1,)))
    lane = lax.broadcasted_iota(jnp.int32, (16, 128), 1) // 32
    for zz in range(N_ROW):
        base = 128 * (zz // 4)
        tile_out = jnp.zeros((16, 128), F32)
        for q in range(N_REP):
            block = new[16 * q : 16 * q + 16, base : base + 128]
            turn = (32 * (q - zz % 4)) % 128
            if turn:
                block = pltpu.roll(block, turn, 1)
            tile_out = jnp.where(lane == q, block, tile_out)
        packed[zz] = tile_out.astype(BF16)
    fac_ref[row] = packed[row]
    last = [
        start(packed.at[peer["row"]], fac_ref.at[row], fs.at[o], fr.at[o], peer) for o, peer in enumerate(row_peers)
    ]
    basis_ref[...] = exact(sk[...].astype(F32), m_ref[...], ((1,), (1,)))
    for copy in last:
        copy.wait_recv()
    for copy in sends:
        copy.wait_send()


def find_range(part, second):
    dma = pltpu.SemaphoreType.DMA
    vmem = pl.BlockSpec(memory_space=pltpu.VMEM)
    rows, rank = part.shape
    counts = (7, 7, 3, 15, 7, 15, 16)
    sems = []
    for count in counts:
        sems += [dma((count,))] * 2
    sems += [dma((2,)), dma((2,)), dma, dma, dma((15,)), dma((15,)), dma((3,)), dma((3,)), dma((15,)), dma((15,))]
    return pl.pallas_call(
        range_kernel,
        out_shape=(
            jax.ShapeDtypeStruct((rows, rank), F32),
            jax.ShapeDtypeStruct((N_ROW, 16, 128), BF16),
        ),
        in_specs=[vmem] * 2,
        out_specs=(vmem,) * 2,
        scratch_shapes=[
            pltpu.VMEM((rows, rank), BF16),
            pltpu.VMEM((N_COL - 1, rows // N_COL, rank), BF16),
            pltpu.VMEM((rows, rank), BF16),
            pltpu.VMEM((rank, rank), F32),
            pltpu.VMEM((rank, rank), F32),
            pltpu.VMEM((3, 16, rank), F32),
            pltpu.VMEM((8, 8, 128), F32),
            pltpu.VMEM((N_ROW, 8, 128), F32),
            pltpu.VMEM((N_ROW, N_REP, 16, rank), F32),
            pltpu.VMEM((2, N_ROW, 16, rank), F32),
            pltpu.VMEM((N_ROW, 16, rank), F32),
            pltpu.VMEM((N_ROW - 1, 16, rank), F32),
            pltpu.VMEM((N_REP, 16, rank), F32),
            pltpu.VMEM((N_ROW, 16, 128), BF16),
            pltpu.VMEM((rank, rank), F32),
            pltpu.VMEM((rank, rank), F32),
        ]
        + sems,
        compiler_params=pltpu.CompilerParams(collective_id=1, has_side_effects=True, vmem_limit_bytes=40 << 20),
        name="find_range",
    )(part, second)


def shards(tokens, out_grad, moment_old, basis_old, factor_old, test_matrix):
    tk, g, f = gather(tokens[0], out_grad[0], factor_old.T.astype(BF16))
    moment, second, part = tile(tk, g, f, moment_old, basis_old, test_matrix)
    basis_new, blocks = find_range(part, second)
    rank = factor_old.shape[1]
    factor_new = blocks.reshape(N_ROW, 16, N_REP, rank).transpose(0, 2, 1, 3).reshape(-1, rank).astype(F32)
    return (moment, basis_new, factor_new)


def solution(mesh):
    placed = (
        P("rep", "col", "row"),
        P("rep", "row", "col"),
        P(("row", "rep"), "col"),
        P(("row", "rep"), None),
        P("col", "row"),
        P("col", None),
    )
    return jax.shard_map(
        shards,
        mesh=mesh,
        in_specs=placed,
        out_specs=(P(("row", "rep"), "col"), P(("row", "rep"), None), P("col", "row")),
        check_vma=False,
    )
```

time: 177 us -> 157 us (0.89)
  Pallas kernels: 167 us -> 147 us
  matrix products: 1.96 us -> 0 us
    pallas_call x4 -> x1, Pallas kernels: 116 us -> 95.7 us  [find_range(): pl.pallas_call(range_kernel, out_shape=(jax.ShapeDtypeStruct((rows, rank)...]
    dot_general x3 -> x0, matrix products: 1.96 us -> none  [the longest x1 1.05 us: shards(): orthonormal = jnp.dot(sketch, inverse.T, precision=lax.Precision.HIGHEST)]
    unnamed x13 -> x12, local copies, waits for them, and re-layouts: 5.74 us -> 6.7 us
where the time goes in v1:
time: 157 us; the launch traced here: 156 us
  Pallas kernels  147 us (94%)
  local copies, waits for them, and re-layouts  6.99 us (4%)
    pallas_call x1, Pallas kernels, find_range(): pl.pallas_call(range_kernel, out_shape=(jax.ShapeDtypeStruct((rows, rank)...  95.7 us
    pallas_call x1, Pallas kernels, gather(): pl.pallas_call(gather_kernel, out_shape=(jax.ShapeDtypeStruct((N_COL, N_R...  47.8 us
    unnamed x12, local copies, waits for them, and re-layouts  6.7 us
    pallas_call x1, Pallas kernels, tile(): pl.pallas_call(tile_kernel, out_shape=(jax.ShapeDtypeStruct((rows, column...  3.74 us

profile of v1, /device:TPU:1, one launch (start us, length us, event | category | flops | bytes accessed | tf_op | source)
XLA Modules:
  0.0 155.8 jit_solution(12346802382835125701)
XLA Ops:
  0.6 0.9 convert_bitcast_fusion.fa_ref
  1.5 0.0 copy-start.3
  1.6 0.8 copy-done.3
  2.4 0.0 copy-start.4
  2.4 0.8 copy-done.4
  3.1 47.8 %gather.1 = (bf16[8,4,32,256]{3,2,1,0:T(8,128)(2,1)S(1)}, bf16[4,16,16,1024]{3,2,1,0:T(8,128)(2,1)S(1)}, bf16[16,2,16,1024]{3,2,1,0:T(8,128)(2,1)S(1)}) custom-call(bf16[32,1024]{1,0:T(8,128)(2,1)S(1)} %bitcast.7, bf16[16,1024]{1,0:T(8,128)(2,1)S(1)} %bitcast.8, bf16[32,1024]{1,0:T(8,128)(2,1)S(1)} %convert_bitcast_fusion.fa_ref), custom_call_target="tpu_custom_call" | custom-call | tf_op jit(solution)/shard_map/gather/pallas_call | solution.py:142
  50.9 0.0 copy-start
  50.9 1.2 copy-done
  52.1 0.0 copy-start.1
  52.1 1.2 copy-done.1
  53.4 0.0 copy-start.2
  53.4 1.0 copy-done.2
  54.4 3.7 %tile.1 = (f32[256,1024]{1,0:T(8,128)}, bf16[256,1024]{1,0:T(8,128)(2,1)S(1)}, f32[256,512]{1,0:T(8,128)S(1)}) custom-call(bf16[8,4,32,256]{3,2,1,0:T(8,128)(2,1)S(1)} %get-tuple-element.11.tk_ref, bf16[4,16,16,1024]{3,2,1,0:T(8,128)(2,1)S(1)} %get-tuple-element.12.g_ref, bf16[16,2,16,1024]{3,2,1,0:T(8,128)(2,1)S(1)} %get-tuple-element.13.f_ref, ...), custom_call_target="tpu_custom_call" | custom-call | tf_op jit(solution)/shard_map/tile/pallas_call | solution.py:191
  58.1 95.7 %find_range.1 = (f32[256,512]{1,0:T(8,128)S(1)}, bf16[16,16,128]{2,1,0:T(8,128)(2,1)S(1)}) custom-call(f32[256,512]{1,0:T(8,128)S(1)} %get-tuple-element.15.part_ref, bf16[256,1024]{1,0:T(8,128)(2,1)S(1)} %get-tuple-element.16.second_ref), custom_call_target="tpu_custom_call" | custom-call | tf_op jit(solution)/shard_map/find_range/pallas_call | solution.py:447
  153.8 0.3 reshape.13
  154.2 0.8 copy.11
  155.0 0.8 copy.13
  (1 shorter events, 0.0 us)
Async XLA Ops:
  1.5 0.8 copy-start.3
  2.4 0.8 copy-start.4
  50.9 1.2 copy-start
  52.1 1.2 copy-start.1
  53.4 1.0 copy-start.2

commit v2 on v1

--- a/solution.py
+++ b/solution.py
@@ -261,7 +261,7 @@
 
 def range_kernel(
     part_ref, second_ref, basis_ref, fac_ref,
-    send_sk, land_sk, sk, gram, out, land1, tiles, land2, z, land_c, land_x, land_z, z_all, packed, m_ref, a_ref,
+    send_sk, land_sk, sk, gram, out, land1, tiles, land2, z, land_c, land_x, land_z, z_all, packed, m_ref, a_ref, away_x, z_half,
     s1, r1, s2, r2, s3, r3, s4, r4, s5, r5, s6, r6, s7, r7, zs1, zr1, zs2, zr2, zs3, zr3, zs4, zr4, fs, fr,
 ):
     row, col, rep = lax.axis_index("row"), lax.axis_index("col"), lax.axis_index("rep")
@@ -331,6 +331,16 @@
         start(z.at[:, 2 * h + 1 - core], land_c.at[h], zs1.at[h], zr1.at[h], sibling) for h in range(2)
     ]
 
+    for copy in z_core:
+        copy.wait_recv()
+
+    def add_core(i, carry):
+        away_x[i] = (land_c[1 - half, i] + z[i, 2 * (1 - half) + core]).astype(BF16)
+        return carry
+
+    lax.fori_loop(0, N_ROW, add_core, 0)
+    z_across = start(away_x, land_x, zs2, zr2, across)
+
     for o in range(N_ROW - 1):
         copies[o].wait_recv()
     total = land2[0]
@@ -346,23 +356,23 @@
         peer = {"row": lax.rem(row + N_ROW + o, N_ROW)}
         copies.append(start(out.at[spot], out.at[spot], s5.at[i], r5.at[i], peer))
 
-    for copy in z_core:
-        copy.wait_recv()
-
-    def add_core(i, carry):
-        for h in range(2):
-            land_c[h, i] = land_c[h, i] + z[i, 2 * h + core]
-        return carry
-
-    lax.fori_loop(0, N_ROW, add_core, 0)
-
     for copy in copies:
         copy.wait_recv()
     here = out.at[pl.ds(strip, 16)]
     copies = [start(here, here, s6.at[i], r6.at[i], peer) for i, peer in enumerate(plane)]
     onward = [start(here, here, s7.at[15], r7.at[15], sibling)]
-    z_across = start(land_c.at[1 - half], land_x, zs2, zr2, across)
+    z_row = []
+
+    def add_across(i, carry):
+        z_half[i] = (land_x[i].astype(F32) + land_c[half, i]) + z[i, 2 * half + core]
+        return carry
+
     for h in range(2):
+        if h == 1:
+            z_across.wait_recv()
+            lax.fori_loop(0, N_ROW, add_across, 0)
+            for o, peer in enumerate(row_peers):
+                z_row.append(start(z_half.at[peer["row"]], land_z.at[o], zs3.at[o], zr3.at[o], peer))
         for o in range(N_COL):
             if h or o:
                 i = h * N_COL + o - 1
@@ -371,16 +381,6 @@
                 copies[i].wait_recv()
                 onward.append(start(there, there, s7.at[i], r7.at[i], sibling))
 
-    z_across.wait_recv()
-
-    def add_across(i, carry):
-        land_x[i] = land_x[i] + land_c[half, i]
-        return carry
-
-    lax.fori_loop(0, N_ROW, add_across, 0)
-    z_row = [
-        start(land_x.at[peer["row"]], land_z.at[o], zs3.at[o], zr3.at[o], peer) for o, peer in enumerate(row_peers)
-    ]
     for copy in onward:
         copy.wait_recv()
 
@@ -395,7 +395,7 @@
         end = (k + 1) * SPAN
         own, rest = slice(k * SPAN, end), slice(end, n)
         if end == n:
-            z_sum = land_x[row]
+            z_sum = z_half[row]
             for o in range(N_ROW - 1):
                 z_row[o].wait_recv()
                 z_sum = z_sum + land_z[o]
@@ -463,12 +463,14 @@
             pltpu.VMEM((N_ROW, 8, 128), F32),
             pltpu.VMEM((N_ROW, N_REP, 16, rank), F32),
             pltpu.VMEM((2, N_ROW, 16, rank), F32),
-            pltpu.VMEM((N_ROW, 16, rank), F32),
+            pltpu.VMEM((N_ROW, 16, rank), BF16),
             pltpu.VMEM((N_ROW - 1, 16, rank), F32),
             pltpu.VMEM((N_REP, 16, rank), F32),
             pltpu.VMEM((N_ROW, 16, 128), BF16),
             pltpu.VMEM((rank, rank), F32),
             pltpu.VMEM((rank, rank), F32),
+            pltpu.VMEM((N_ROW, 16, rank), BF16),
+            pltpu.VMEM((N_ROW, 16, rank), F32),
         ]
         + sems,
         compiler_params=pltpu.CompilerParams(collective_id=1, has_side_effects=True, vmem_limit_bytes=40 << 20),

time: 157 us -> 146 us (0.930); the launches traced: 156 us -> 143 us
  Pallas kernels: 147 us -> 134 us
    pallas_call x1, Pallas kernels: 95.7 us -> 82.8 us  [find_range(): pl.pallas_call(range_kernel, out_shape=(jax.ShapeDtypeStruct((rows, rank)...]
where the time goes in v2:
time: 146 us; the launch traced here: 143 us
  Pallas kernels  134 us (92%)
  local copies, waits for them, and re-layouts  6.99 us (5%)
    pallas_call x1, Pallas kernels, find_range(): pl.pallas_call(range_kernel, out_shape=(jax.ShapeDtypeStruct((rows, rank)...  82.8 us
    pallas_call x1, Pallas kernels, gather(): pl.pallas_call(gather_kernel, out_shape=(jax.ShapeDtypeStruct((N_COL, N_R...  47.8 us
    unnamed x12, local copies, waits for them, and re-layouts  6.7 us
    pallas_call x1, Pallas kernels, tile(): pl.pallas_call(tile_kernel, out_shape=(jax.ShapeDtypeStruct((rows, column...  3.74 us

profile of v2, /device:TPU:1, one launch (start us, length us, event | category | flops | bytes accessed | tf_op | source)
XLA Modules:
  0.0 142.9 jit_solution(4372947780082442069)
XLA Ops:
  0.6 0.9 convert_bitcast_fusion.fa_ref
  1.5 0.0 copy-start.3
  1.6 0.8 copy-done.3
  2.4 0.0 copy-start.4
  2.4 0.8 copy-done.4
  3.1 47.8 %gather.1 = (bf16[8,4,32,256]{3,2,1,0:T(8,128)(2,1)S(1)}, bf16[4,16,16,1024]{3,2,1,0:T(8,128)(2,1)S(1)}, bf16[16,2,16,1024]{3,2,1,0:T(8,128)(2,1)S(1)}) custom-call(bf16[32,1024]{1,0:T(8,128)(2,1)S(1)} %bitcast.7, bf16[16,1024]{1,0:T(8,128)(2,1)S(1)} %bitcast.8, bf16[32,1024]{1,0:T(8,128)(2,1)S(1)} %convert_bitcast_fusion.fa_ref), custom_call_target="tpu_custom_call" | custom-call | tf_op jit(solution)/shard_map/gather/pallas_call | solution.py:142
  50.9 0.0 copy-start
  50.9 1.2 copy-done
  52.1 0.0 copy-start.1
  52.1 1.2 copy-done.1
  53.4 0.0 copy-start.2
  53.4 1.0 copy-done.2
  54.4 3.7 %tile.1 = (f32[256,1024]{1,0:T(8,128)}, bf16[256,1024]{1,0:T(8,128)(2,1)S(1)}, f32[256,512]{1,0:T(8,128)S(1)}) custom-call(bf16[8,4,32,256]{3,2,1,0:T(8,128)(2,1)S(1)} %get-tuple-element.11.tk_ref, bf16[4,16,16,1024]{3,2,1,0:T(8,128)(2,1)S(1)} %get-tuple-element.12.g_ref, bf16[16,2,16,1024]{3,2,1,0:T(8,128)(2,1)S(1)} %get-tuple-element.13.f_ref, ...), custom_call_target="tpu_custom_call" | custom-call | tf_op jit(solution)/shard_map/tile/pallas_call | solution.py:191
  58.1 82.8 %find_range.1 = (f32[256,512]{1,0:T(8,128)S(1)}, bf16[16,16,128]{2,1,0:T(8,128)(2,1)S(1)}) custom-call(f32[256,512]{1,0:T(8,128)S(1)} %get-tuple-element.15.part_ref, bf16[256,1024]{1,0:T(8,128)(2,1)S(1)} %get-tuple-element.16.second_ref), custom_call_target="tpu_custom_call" | custom-call | tf_op jit(solution)/shard_map/find_range/pallas_call | solution.py:447
  141.0 0.3 reshape.13
  141.3 0.8 copy.11
  142.1 0.8 copy.13
  (1 shorter events, 0.0 us)
Async XLA Ops:
  1.5 0.8 copy-start.3
  2.4 0.8 copy-start.4
  50.9 1.2 copy-start
  52.1 1.2 copy-start.1
  53.4 1.0 copy-start.2

commit v3 on v2

--- a/solution.py
+++ b/solution.py
@@ -31,161 +31,163 @@
     return [{axis: lax.rem(me + o, size)} for o in range(1, size)]
 
 
-def gather_kernel(tok_ref, og_ref, fa_ref, tk_ref, g_ref, f_ref, rs, rr, ss, sr, xs, xr, ts, tr, cs, cr):
+HOPS = (
+    (0, 4), (0, 8), (0, 12), (0, 1), (0, -1), (0, 2),
+    (4, 1), (4, -1), (4, 2), (4, -2),
+    (8, 1), (8, -1), (8, -2),
+    (12, 1), (12, -1),
+)
+NEAR = ((0, 1, 2), (3, 6, 10, 13), (4, 7, 11, 14), (5, 8, 9, 12))
+
+
+def tile_kernel(
+    tok_ref, og_ref, fa_ref, moment_ref, basis_ref, test_ref, new_ref, second_ref, part_ref,
+    tk, g, f, old_f, old_m, old_b, test, high, low, zs, zr, xs, xr, ss, sr, ts, tr, cs, cr, local,
+):
     row, col, rep = lax.axis_index("row"), lax.axis_index("col"), lax.axis_index("rep")
     half, core = rep // 2, lax.rem(rep, 2)
     across = (1 - half) * 2 + core
     sibling = half * 2 + 1 - core
+    corner = (1 - half) * 2 + 1 - core
     rep_peers = others("rep", N_REP)
     col_peers = others("col", N_COL)
-    sides = ({"row": lax.rem(row + 1, N_ROW)}, {"row": lax.rem(row + N_ROW - 1, N_ROW)})
+
+    def at(offset):
+        return lax.rem(row + N_ROW + offset, N_ROW)
+
     wide = tok_ref.shape[1] // N_REP
     part = pl.ds(pl.multiple_of(rep * wide, wide), wide)
-    g_ref[rep, row] = og_ref[...]
-    f_ref[row, 0] = fa_ref[:16]
-    f_ref[row, 1] = fa_ref[16:]
-    tk_ref[col, rep] = tok_ref[:, part]
-    greet(rep_peers + col_peers + list(sides))
-
-    def slot(stream, z, c=core):
-        if stream == 2:
-            return f_ref.at[z, c]
-        return g_ref.at[(half if stream == 0 else 1 - half) * 2 + c, z]
-
-    def ring(stream, side, step):
-        z = lax.rem(row + N_ROW + (1 - step if side == 0 else step - 1), N_ROW)
-        return remote(slot(stream, z), slot(stream, z), rs.at[stream, side, step], rr.at[stream, side, step], sides[side])
-
-    def arrival(stream, side, step):
-        z = lax.rem(row + N_ROW + (-step if side == 0 else step), N_ROW)
-        return remote(slot(stream, z), slot(stream, z), rs.at[stream, side, step], rr.at[stream, side, step], sides[side])
-
-    def hand(stream, index, c=core):
-        z = lax.rem(row + N_ROW + jnp.where(index <= 8, -index, index - 8), N_ROW)
-        return remote(slot(stream, z, c), slot(stream, z, c), ss.at[stream, index], sr.at[stream, index], {"rep": sibling})
-
-    swap = remote(slot(0, row), slot(0, row), xs, xr, {"rep": across})
-    swap.start()
-    for stream in (0, 2):
-        for side in range(2):
-            ring(stream, side, 1).start()
+    own = [
+        pltpu.make_async_copy(og_ref, g.at[rep, row // 4, lax.rem(row, 4)], local.at[0]),
+        pltpu.make_async_copy(fa_ref, old_f, local.at[1]),
+        pltpu.make_async_copy(tok_ref.at[:, part], tk.at[col, rep], local.at[2]),
+        pltpu.make_async_copy(moment_ref, old_m, local.at[3]),
+        pltpu.make_async_copy(basis_ref, old_b, local.at[4]),
+        pltpu.make_async_copy(test_ref, test, local.at[5]),
+    ]
+    for copy in own:
+        copy.start()
+    greet(rep_peers + col_peers + [{"row": at(o)} for o in (1, -1, 2, -2, 4, 8, 12)])
+
+    def slot(stream, z):
+        if stream:
+            return f.at[z // 4, lax.rem(z, 4), core]
+        return g.at[rep, z // 4, lax.rem(z, 4)]
+
+    def hop(stream, i, arriving=False):
+        d, o = HOPS[i]
+        here = slot(stream, at(d - o if arriving else d))
+        return remote(here, here, zs.at[stream, i], zr.at[stream, i], {"row": at(o)})
+
+    classes = [lax.rem(row + 4 + o, 4) for o in (0, -1, 1, 2)]
+
+    def over(j, arriving=False):
+        here = g.at[across if arriving else rep, :, classes[j]]
+        return remote(here, here, xs.at[j], xr.at[j], {"rep": across})
+
+    def hand(kind, j, arriving=False):
+        if kind == 2:
+            here = f.at[:, classes[j], (1 - core) if arriving else core]
+        elif kind == 1:
+            here = g.at[corner if arriving else across, :, classes[j]]
+        else:
+            here = g.at[sibling if arriving else rep, :, classes[j]]
+        return remote(here, here, ss.at[kind, j], sr.at[kind, j], {"rep": sibling})
+
+    sends = []
+
+    def go(copy):
+        copy.start()
+        sends.append(copy)
+
+    own[0].wait()
+    for i in range(6):
+        go(hop(0, i))
     first = []
     for o, peer in enumerate(rep_peers):
-        start = pl.multiple_of(peer["rep"] * wide, wide)
-        copy = remote(tok_ref.at[:, pl.ds(start, wide)], tk_ref.at[col, rep], ts.at[o], tr.at[o], peer)
-        copy.start()
+        there = pl.ds(pl.multiple_of(peer["rep"] * wide, wide), wide)
+        copy = remote(tok_ref.at[:, there], tk.at[col, rep], ts.at[o], tr.at[o], peer)
+        go(copy)
         first.append(copy)
-    hand(0, 0).start()
-    swap.wait_recv()
-    for side in range(2):
-        ring(1, side, 1).start()
-    hand(1, 0).start()
-    for copy in first:
-        copy.wait_recv()
-    second = []
-    for o, peer in enumerate(col_peers):
-        copy = remote(tk_ref.at[col], tk_ref.at[col], cs.at[o], cr.at[o], peer)
-        copy.start()
-        second.append(copy)
-
-    def step(s, carry):
-        for stream in (0, 2, 1):
-            arrival(stream, 0, s).wait_recv()
-            ring(stream, 0, s + 1).start()
-            hand(stream, s).start()
-            arrival(stream, 1, s).wait_recv()
-
-            @pl.when(s < 7)
-            def _():
-                ring(stream, 1, s + 1).start()
-
-            hand(stream, s + 8).start()
-        return carry
-
-    lax.fori_loop(1, 8, step, 0)
-    for stream in (0, 2, 1):
-        arrival(stream, 0, 8).wait_recv()
-        hand(stream, 8).start()
+    own[1].wait()
+    f[row // 4, lax.rem(row, 4), core] = old_f[pl.ds(pl.multiple_of(16 * core, 16), 16)].astype(BF16)
+    for i in range(6):
+        go(hop(1, i))
+    for stream in range(2):
+        for i, onward in ((0, (13, 14)), (2, (6, 7, 8, 9)), (1, (10, 11, 12))):
+            hop(stream, i, True).wait_recv()
+            for k in onward:
+                go(hop(stream, k))
+        if stream == 0:
+            go(over(0))
+            go(hand(0, 0))
+            own[2].wait()
+            for copy in first:
+                copy.wait_recv()
+            second = []
+            for o, peer in enumerate(col_peers):
+                copy = remote(tk.at[col], tk.at[col], cs.at[o], cr.at[o], peer)
+                go(copy)
+                second.append(copy)
+        else:
+            go(hand(2, 0))
+    for j in (1, 2, 3):
+        for i in NEAR[j]:
+            hop(0, i, True).wait_recv()
+        go(over(j))
+        go(hand(0, j))
+    for j in (0, 1):
+        over(j, True).wait_recv()
+        go(hand(1, j))
+    for j in (1, 2, 3):
+        for i in NEAR[j]:
+            hop(1, i, True).wait_recv()
+        go(hand(2, j))
+    for j in (2, 3):
+        over(j, True).wait_recv()
+        go(hand(1, j))
+    for copy in own[3:]:
+        copy.wait()
+    high[...] = old_b[...].astype(BF16)
+    low[...] = (old_b[...] - high[...].astype(F32)).astype(BF16)
+    part_ref[...] = jnp.zeros_like(part_ref)
     for copy in second:
         copy.wait_recv()
-
-    def finish(i, carry):
-        for stream in range(3):
-            hand(stream, i, 1 - core).wait_recv()
-            hand(stream, i).wait_send()
-        return carry
-
-    for stream in range(2):
-        hand(stream, 0, 1 - core).wait_recv()
-        hand(stream, 0).wait_send()
-    lax.fori_loop(1, 16, finish, 0)
-
-    def drain(s, carry):
-        for stream in range(3):
-            for side in range(2):
-                ring(stream, side, s).wait_send()
-        return carry
-
-    lax.fori_loop(1, 8, drain, 0)
-    for stream in range(3):
-        ring(stream, 0, 8).wait_send()
-    swap.wait_send()
-    for copy in first + second:
-        copy.wait_send()
-
-
-def gather(tokens, out_grad, factor):
-    dma = pltpu.SemaphoreType.DMA
-    vmem = pl.BlockSpec(memory_space=pltpu.VMEM)
-    depth, wide = tokens.shape[0], tokens.shape[1] // N_REP
-    tall, across = out_grad.shape
-    return pl.pallas_call(
-        gather_kernel,
-        out_shape=(
-            jax.ShapeDtypeStruct((N_COL, N_REP, depth, wide), BF16),
-            jax.ShapeDtypeStruct((N_REP, N_ROW, tall, across), BF16),
-            jax.ShapeDtypeStruct((N_ROW, 2, factor.shape[0] // 2, across), BF16),
-        ),
-        in_specs=[vmem] * 3,
-        out_specs=(vmem,) * 3,
-        scratch_shapes=[
-            dma((3, 2, 9)), dma((3, 2, 9)), dma((3, 16)), dma((3, 16)), dma, dma,
-            dma((3,)), dma((3,)), dma((7,)), dma((7,)),
-        ],
-        compiler_params=pltpu.CompilerParams(collective_id=4, has_side_effects=True, vmem_limit_bytes=12 << 20),
-        name="gather",
-    )(tokens, out_grad, factor)
-
-
-def tile_kernel(tk_ref, g_ref, f_ref, moment_ref, basis_ref, test_ref, new_ref, second_ref, part_ref, high, low):
+    for j in range(4):
+        for kind in range(3):
+            hand(kind, j, True).wait_recv()
+
     step = 256
-    high[...] = basis_ref[...].astype(BF16)
-    low[...] = (basis_ref[...] - high[...].astype(F32)).astype(BF16)
-    rank = basis_ref.shape[1]
-    part_ref[...] = jnp.zeros_like(part_ref)
+    rank = old_b.shape[1]
 
     def columns(i, carry):
         here = pl.ds(pl.multiple_of(i * step, step), step)
         gradient = jnp.zeros((new_ref.shape[0], step), F32)
         for b in range(N_REP):
-            left = tk_ref[:, b].reshape(-1, tk_ref.shape[3])
-            right = g_ref[b, :, :, here].reshape(-1, step)
+            left = tk[:, b].reshape(-1, wide)
+            right = g[b, :, :, :, here].reshape(-1, step)
             piece = lax.dot_general(left, right, (((0,), (0,)), ((), ())), preferred_element_type=F32)
             gradient = gradient + piece.astype(BF16).astype(F32)
-        new_ref[:, here] = 0.9 * moment_ref[:, here] + 0.1 * gradient
-        factor = f_ref[:, :, :, here].reshape(rank, step)
+        new_ref[:, here] = 0.9 * old_m[:, here] + 0.1 * gradient
+        factor = f[:, :, :, :, here].reshape(rank, step)
         previous = jnp.dot(high[...], factor, preferred_element_type=F32)
         previous = previous + jnp.dot(low[...], factor, preferred_element_type=F32)
-        second = (0.95 * previous + 0.05 * gradient * gradient).astype(BF16)
-        second_ref[:, here] = second
-        part_ref[...] += jnp.dot(second, test_ref[here], preferred_element_type=F32)
+        second_tile = (0.95 * previous + 0.05 * gradient * gradient).astype(BF16)
+        second_ref[:, here] = second_tile
+        part_ref[...] += jnp.dot(second_tile, test[here], preferred_element_type=F32)
         return carry
 
     lax.fori_loop(0, new_ref.shape[1] // step, columns, 0)
-
-
-def tile(tk, g, f, moment_old, basis_old, test_matrix):
+    for copy in sends:
+        copy.wait_send()
+
+
+def tile(tokens, out_grad, factor, moment_old, basis_old, test_matrix):
+    dma = pltpu.SemaphoreType.DMA
     vmem = pl.BlockSpec(memory_space=pltpu.VMEM)
+    hbm = pl.BlockSpec(memory_space=pltpu.HBM)
+    depth, wide = tokens.shape[0], tokens.shape[1] // N_REP
+    tall = out_grad.shape[0]
     rows, columns = moment_old.shape
     rank = basis_old.shape[1]
     return pl.pallas_call(
@@ -195,12 +197,26 @@
             jax.ShapeDtypeStruct((rows, columns), BF16),
             jax.ShapeDtypeStruct((rows, rank), F32),
         ),
-        in_specs=[vmem] * 6,
+        in_specs=[hbm] * 6,
         out_specs=(vmem,) * 3,
-        scratch_shapes=[pltpu.VMEM((rows, rank), BF16)] * 2,
-        compiler_params=pltpu.CompilerParams(vmem_limit_bytes=20 << 20),
+        scratch_shapes=[
+            pltpu.VMEM((N_COL, N_REP, depth, wide), BF16),
+            pltpu.VMEM((N_REP, 4, 4, tall, columns), BF16),
+            pltpu.VMEM((4, 4, 2, factor.shape[0] // 2, columns), BF16),
+            pltpu.VMEM(factor.shape, F32),
+            pltpu.VMEM(moment_old.shape, F32),
+            pltpu.VMEM(basis_old.shape, F32),
+            pltpu.VMEM(test_matrix.shape, BF16),
+            pltpu.VMEM((rows, rank), BF16),
+            pltpu.VMEM((rows, rank), BF16),
+            dma((2, 15)), dma((2, 15)), dma((4,)), dma((4,)), dma((3, 4)), dma((3, 4)),
+            dma((3,)), dma((3,)), dma((7,)), dma((7,)), dma((6,)),
+        ],
+        compiler_params=pltpu.CompilerParams(
+            collective_id=4, has_side_effects=True, vmem_limit_bytes=54 << 20
+        ),
         name="tile",
-    )(tk, g, f, moment_old, basis_old, test_matrix)
+    )(tokens, out_grad, factor, moment_old, basis_old, test_matrix)
 
 
 SPAN = 128
@@ -479,8 +495,7 @@
 
 
 def shards(tokens, out_grad, moment_old, basis_old, factor_old, test_matrix):
-    tk, g, f = gather(tokens[0], out_grad[0], factor_old.T.astype(BF16))
-    moment, second, part = tile(tk, g, f, moment_old, basis_old, test_matrix)
+    moment, second, part = tile(tokens[0], out_grad[0], factor_old.T, moment_old, basis_old, test_matrix)
     basis_new, blocks = find_range(part, second)
     rank = factor_old.shape[1]
     factor_new = blocks.reshape(N_ROW, 16, N_REP, rank).transpose(0, 2, 1, 3).reshape(-1, rank).astype(F32)

time: 146 us -> 147 us (level); the launches traced: 143 us -> 147 us
  Pallas kernels: 134 us -> 141 us
  local copies, waits for them, and re-layouts: 6.99 us -> 5.04 us
    pallas_call x1, Pallas kernels: 3.74 us -> 53.9 us  [tile(): pl.pallas_call(tile_kernel, out_shape=(jax.ShapeDtypeStruct((rows, column...]
    pallas_call x1 -> x0, Pallas kernels: 47.8 us -> none  [gather(): pl.pallas_call(gather_kernel, out_shape=(jax.ShapeDtypeStruct((N_COL, N_R...]
    pallas_call x1, Pallas kernels: 82.8 us -> 86.9 us  [find_range(): pl.pallas_call(range_kernel, out_shape=(jax.ShapeDtypeStruct((rows, rank)...]
    unnamed x12 -> x9, local copies, waits for them, and re-layouts: 6.7 us -> 4.75 us
where the time goes in v3:
time: 147 us
  Pallas kernels  141 us (96%)
  local copies, waits for them, and re-layouts  5.04 us (3%)
    pallas_call x1, Pallas kernels, find_range(): pl.pallas_call(range_kernel, out_shape=(jax.ShapeDtypeStruct((rows, rank)...  86.9 us
    pallas_call x1, Pallas kernels, tile(): pl.pallas_call(tile_kernel, out_shape=(jax.ShapeDtypeStruct((rows, column...  53.9 us
    unnamed x9, local copies, waits for them, and re-layouts  4.75 us

profile of v3, /device:TPU:1, one launch (start us, length us, event | category | flops | bytes accessed | tf_op | source)
XLA Modules:
  0.0 146.5 jit_solution(5145736929559695347)
XLA Ops:
  0.6 53.9 %tile.1 = (f32[256,1024]{1,0:T(8,128)}, bf16[256,1024]{1,0:T(8,128)(2,1)}, f32[256,512]{1,0:T(8,128)}) custom-call(bf16[32,1024]{1,0:T(8,128)(2,1)} %bitcast.8, bf16[16,1024]{1,0:T(8,128)(2,1)} %bitcast.9, f32[32,1024]{1,0:T(8,128)} %bitcast.7, f32[256,1024]{1,0:T(8,128)} %moment_ref.1, f32[256,512]{1,0:T(8,128)} %basis_ref.1, bf16[1024,512]{1,0:T(8,128)(2,1)} %test_ref.1), custom_call_target="tpu_custom_call" | custom-call | tf_op jit(solution)/shard_map/tile/pallas_call | solution.py:193
  54.5 0.0 copy-start
  54.5 1.0 copy-done
  55.6 0.0 copy-start.1
  55.6 1.0 copy-done.1
  56.6 86.9 %find_range.1 = (f32[256,512]{1,0:T(8,128)S(1)}, bf16[16,16,128]{2,1,0:T(8,128)(2,1)S(1)}) custom-call(f32[256,512]{1,0:T(8,128)S(1)} %copy-done.1, bf16[256,1024]{1,0:T(8,128)(2,1)S(1)} %copy-done), custom_call_target="tpu_custom_call" | custom-call | tf_op jit(solution)/shard_map/find_range/pallas_call | solution.py:463
  143.5 0.0 copy-start.2
  143.6 0.3 reshape.13
  143.9 0.8 copy.11
  144.7 0.1 copy-done.2
  144.8 1.0 copy.14
  145.7 0.8 copy.15
  (1 shorter events, 0.0 us)
Async XLA Ops:
  54.5 1.0 copy-start
  55.6 1.0 copy-start.1
  143.5 1.2 copy-start.2

commit v4 on v3

--- a/solution.py
+++ b/solution.py
@@ -67,7 +67,12 @@
     ]
     for copy in own:
         copy.start()
-    greet(rep_peers + col_peers + [{"row": at(o)} for o in (1, -1, 2, -2, 4, 8, 12)])
+    plane = []
+    for h in range(2):
+        for o in range(N_COL):
+            if h or o:
+                plane.append({"col": lax.rem(col + o, N_COL), "rep": lax.rem(half + h, 2) * 2 + core})
+    greet(rep_peers + others("row", N_ROW) + plane)
 
     def slot(stream, z):
         if stream:
@@ -182,43 +187,6 @@
         copy.wait_send()
 
 
-def tile(tokens, out_grad, factor, moment_old, basis_old, test_matrix):
-    dma = pltpu.SemaphoreType.DMA
-    vmem = pl.BlockSpec(memory_space=pltpu.VMEM)
-    hbm = pl.BlockSpec(memory_space=pltpu.HBM)
-    depth, wide = tokens.shape[0], tokens.shape[1] // N_REP
-    tall = out_grad.shape[0]
-    rows, columns = moment_old.shape
-    rank = basis_old.shape[1]
-    return pl.pallas_call(
-        tile_kernel,
-        out_shape=(
-            jax.ShapeDtypeStruct((rows, columns), F32),
-            jax.ShapeDtypeStruct((rows, columns), BF16),
-            jax.ShapeDtypeStruct((rows, rank), F32),
-        ),
-        in_specs=[hbm] * 6,
-        out_specs=(vmem,) * 3,
-        scratch_shapes=[
-            pltpu.VMEM((N_COL, N_REP, depth, wide), BF16),
-            pltpu.VMEM((N_REP, 4, 4, tall, columns), BF16),
-            pltpu.VMEM((4, 4, 2, factor.shape[0] // 2, columns), BF16),
-            pltpu.VMEM(factor.shape, F32),
-            pltpu.VMEM(moment_old.shape, F32),
-            pltpu.VMEM(basis_old.shape, F32),
-            pltpu.VMEM(test_matrix.shape, BF16),
-            pltpu.VMEM((rows, rank), BF16),
-            pltpu.VMEM((rows, rank), BF16),
-            dma((2, 15)), dma((2, 15)), dma((4,)), dma((4,)), dma((3, 4)), dma((3, 4)),
-            dma((3,)), dma((3,)), dma((7,)), dma((7,)), dma((6,)),
-        ],
-        compiler_params=pltpu.CompilerParams(
-            collective_id=4, has_side_effects=True, vmem_limit_bytes=54 << 20
-        ),
-        name="tile",
-    )(tokens, out_grad, factor, moment_old, basis_old, test_matrix)
-
-
 SPAN = 128
 
 
@@ -240,7 +208,8 @@
         inverse = [None] * 8
         f = [[None] * 8 for _ in range(8)]
         for m in range(8):
-            inverse[m] = 1.0 / s[m][m]
+            guess = pl.reciprocal(s[m][m], approx=True)
+            inverse[m] = guess * (2.0 - s[m][m] * guess)
             for i in range(m + 1, 8):
                 f[i][m] = s[i][m] * inverse[m]
             for i in range(m + 1, 8):
@@ -301,7 +270,6 @@
         return copy
 
     send_sk[...] = part_ref[...].astype(BF16)
-    greet(rep_peers + row_peers + plane)
     rows = part_ref.shape[0] // N_COL
     mine = pl.ds(pl.multiple_of(col * rows, rows), rows)
     copies = []
@@ -451,24 +419,48 @@
         copy.wait_send()
 
 
-def find_range(part, second):
+def whole_kernel(*refs):
+    inputs, new_ref, basis_ref, fac_ref = refs[:6], refs[6], refs[7], refs[8]
+    second, part = refs[9:11]
+    tile_kernel(*inputs, new_ref, second, part, *refs[11:31])
+    range_kernel(part, second, basis_ref, fac_ref, *refs[31:])
+
+
+def whole(tokens, out_grad, factor, moment_old, basis_old, test_matrix):
     dma = pltpu.SemaphoreType.DMA
     vmem = pl.BlockSpec(memory_space=pltpu.VMEM)
-    rows, rank = part.shape
-    counts = (7, 7, 3, 15, 7, 15, 16)
+    hbm = pl.BlockSpec(memory_space=pltpu.HBM)
+    depth, wide = tokens.shape[0], tokens.shape[1] // N_REP
+    tall = out_grad.shape[0]
+    rows, columns = moment_old.shape
+    rank = basis_old.shape[1]
     sems = []
-    for count in counts:
+    for count in (7, 7, 3, 15, 7, 15, 16):
         sems += [dma((count,))] * 2
     sems += [dma((2,)), dma((2,)), dma, dma, dma((15,)), dma((15,)), dma((3,)), dma((3,)), dma((15,)), dma((15,))]
     return pl.pallas_call(
-        range_kernel,
+        whole_kernel,
         out_shape=(
+            jax.ShapeDtypeStruct((rows, columns), F32),
             jax.ShapeDtypeStruct((rows, rank), F32),
             jax.ShapeDtypeStruct((N_ROW, 16, 128), BF16),
         ),
-        in_specs=[vmem] * 2,
-        out_specs=(vmem,) * 2,
+        in_specs=[hbm] * 6,
+        out_specs=(vmem,) * 3,
         scratch_shapes=[
+            pltpu.VMEM((rows, columns), BF16),
+            pltpu.VMEM((rows, rank), F32),
+            pltpu.VMEM((N_COL, N_REP, depth, wide), BF16),
+            pltpu.VMEM((N_REP, 4, 4, tall, columns), BF16),
+            pltpu.VMEM((4, 4, 2, factor.shape[0] // 2, columns), BF16),
+            pltpu.VMEM(factor.shape, F32),
+            pltpu.VMEM(moment_old.shape, F32),
+            pltpu.VMEM(basis_old.shape, F32),
+            pltpu.VMEM(test_matrix.shape, BF16),
+            pltpu.VMEM((rows, rank), BF16),
+            pltpu.VMEM((rows, rank), BF16),
+            dma((2, 15)), dma((2, 15)), dma((4,)), dma((4,)), dma((3, 4)), dma((3, 4)),
+            dma((3,)), dma((3,)), dma((7,)), dma((7,)), dma((6,)),
             pltpu.VMEM((rows, rank), BF16),
             pltpu.VMEM((N_COL - 1, rows // N_COL, rank), BF16),
             pltpu.VMEM((rows, rank), BF16),
@@ -489,14 +481,13 @@
             pltpu.VMEM((N_ROW, 16, rank), F32),
         ]
         + sems,
-        compiler_params=pltpu.CompilerParams(collective_id=1, has_side_effects=True, vmem_limit_bytes=40 << 20),
-        name="find_range",
-    )(part, second)
+        compiler_params=pltpu.CompilerParams(collective_id=1, has_side_effects=True, vmem_limit_bytes=54 << 20),
+        name="whole",
+    )(tokens, out_grad, factor, moment_old, basis_old, test_matrix)
 
 
 def shards(tokens, out_grad, moment_old, basis_old, factor_old, test_matrix):
-    moment, second, part = tile(tokens[0], out_grad[0], factor_old.T, moment_old, basis_old, test_matrix)
-    basis_new, blocks = find_range(part, second)
+    moment, basis_new, blocks = whole(tokens[0], out_grad[0], factor_old.T, moment_old, basis_old, test_matrix)
     rank = factor_old.shape[1]
     factor_new = blocks.reshape(N_ROW, 16, N_REP, rank).transpose(0, 2, 1, 3).reshape(-1, rank).astype(F32)
     return (moment, basis_new, factor_new)

time: 147 us -> 141 us (0.959)
  Pallas kernels: 141 us -> 136 us
    pallas_call x2 -> x1, Pallas kernels: 141 us -> 136 us  [whole(): pl.pallas_call(whole_kernel, out_shape=(jax.ShapeDtypeStruct((rows, colum...]
    unnamed x9 -> x7, local copies, waits for them, and re-layouts: 4.75 us -> 3.03 us
where the time goes in v4:
time: 141 us
  Pallas kernels  136 us (96%)
  local copies, waits for them, and re-layouts  4.24 us (3%)
    pallas_call x1, Pallas kernels, whole(): pl.pallas_call(whole_kernel, out_shape=(jax.ShapeDtypeStruct((rows, colum...  136 us
    unnamed x7, local copies, waits for them, and re-layouts  3.03 us

profile of v4, /device:TPU:1, one launch (start us, length us, event | category | flops | bytes accessed | tf_op | source)
XLA Modules:
  0.0 140.9 jit_solution(16260435257011500416)
XLA Ops:
  0.6 136.0 %whole.1 = (f32[256,1024]{1,0:T(8,128)}, f32[256,512]{1,0:T(8,128)}, bf16[16,16,128]{2,1,0:T(8,128)(2,1)}) custom-call(bf16[32,1024]{1,0:T(8,128)(2,1)} %bitcast.8, bf16[16,1024]{1,0:T(8,128)(2,1)} %bitcast.9, f32[32,1024]{1,0:T(8,128)} %bitcast.7, f32[256,1024]{1,0:T(8,128)} %refs_3_.1, f32[256,512]{1,0:T(8,128)} %refs_4_.1, bf16[1024,512]{1,0:T(8,128)(2,1)} %refs_5_.1), custom_call_target="tpu_custom_call" | custom-call | tf_op jit(solution)/shard_map/whole/pallas_call | solution.py:441
  136.6 0.0 copy-start
  136.6 1.2 reshape.13
  137.9 0.8 copy.11
  138.7 0.0 copy-done
  138.7 0.0 copy-start.1
  138.7 1.0 copy.14
  139.7 0.4 copy-done.1
  140.1 0.8 copy.15
  (1 shorter events, 0.0 us)
Async XLA Ops:
  136.6 2.1 %copy-start = (f32[256,1024]{1,0:T(8,128)S(1)}, f32[256,1024]{1,0:T(8,128)}, u32[]{:S(2)}) copy-start(f32[256,1024]{1,0:T(8,128)} %get-tuple-element.15) | copy-start | bytes 3145732
  138.7 1.4 copy-start.1

commit v5 on v4

--- a/solution.py
+++ b/solution.py
@@ -116,31 +116,32 @@
         first.append(copy)
     own[1].wait()
     f[row // 4, lax.rem(row, 4), core] = old_f[pl.ds(pl.multiple_of(16 * core, 16), 16)].astype(BF16)
-    for i in range(6):
-        go(hop(1, i))
-    for stream in range(2):
+    def pass_on(stream):
         for i, onward in ((0, (13, 14)), (2, (6, 7, 8, 9)), (1, (10, 11, 12))):
             hop(stream, i, True).wait_recv()
             for k in onward:
                 go(hop(stream, k))
-        if stream == 0:
-            go(over(0))
-            go(hand(0, 0))
-            own[2].wait()
-            for copy in first:
-                copy.wait_recv()
-            second = []
-            for o, peer in enumerate(col_peers):
-                copy = remote(tk.at[col], tk.at[col], cs.at[o], cr.at[o], peer)
-                go(copy)
-                second.append(copy)
-        else:
-            go(hand(2, 0))
+
+    pass_on(0)
+    for i in range(6):
+        go(hop(1, i))
+    go(over(0))
+    go(hand(0, 0))
+    own[2].wait()
+    for copy in first:
+        copy.wait_recv()
+    second = []
+    for o, peer in enumerate(col_peers):
+        copy = remote(tk.at[col], tk.at[col], cs.at[o], cr.at[o], peer)
+        go(copy)
+        second.append(copy)
     for j in (1, 2, 3):
         for i in NEAR[j]:
             hop(0, i, True).wait_recv()
         go(over(j))
         go(hand(0, j))
+    pass_on(1)
+    go(hand(2, 0))
     for j in (0, 1):
         over(j, True).wait_recv()
         go(hand(1, j))

time: 141 us -> 137 us (0.972)
  Pallas kernels: 136 us -> 131 us
    pallas_call x1, Pallas kernels: 136 us -> 131 us  [whole(): pl.pallas_call(whole_kernel, out_shape=(jax.ShapeDtypeStruct((rows, colum...]
where the time goes in v5:
time: 137 us; the launch traced here: 136 us
  Pallas kernels  131 us (96%)
  local copies, waits for them, and re-layouts  4.24 us (3%)
    pallas_call x1, Pallas kernels, whole(): pl.pallas_call(whole_kernel, out_shape=(jax.ShapeDtypeStruct((rows, colum...  131 us
    unnamed x7, local copies, waits for them, and re-layouts  3.03 us

profile of v5, /device:TPU:1, one launch (start us, length us, event | category | flops | bytes accessed | tf_op | source)
XLA Modules:
  0.0 136.4 jit_solution(16798318777811310469)
XLA Ops:
  0.6 131.5 %whole.1 = (f32[256,1024]{1,0:T(8,128)}, f32[256,512]{1,0:T(8,128)}, bf16[16,16,128]{2,1,0:T(8,128)(2,1)}) custom-call(bf16[32,1024]{1,0:T(8,128)(2,1)} %bitcast.8, bf16[16,1024]{1,0:T(8,128)(2,1)} %bitcast.9, f32[32,1024]{1,0:T(8,128)} %bitcast.7, f32[256,1024]{1,0:T(8,128)} %refs_3_.1, f32[256,512]{1,0:T(8,128)} %refs_4_.1, bf16[1024,512]{1,0:T(8,128)(2,1)} %refs_5_.1), custom_call_target="tpu_custom_call" | custom-call | tf_op jit(solution)/shard_map/whole/pallas_call | solution.py:442
  132.1 0.0 copy-start
  132.1 1.2 reshape.13
  133.4 0.8 copy.11
  134.2 0.0 copy-done
  134.2 0.0 copy-start.1
  134.2 1.0 copy.14
  135.2 0.4 copy-done.1
  135.6 0.8 copy.15
  (1 shorter events, 0.0 us)
Async XLA Ops:
  132.1 2.1 %copy-start = (f32[256,1024]{1,0:T(8,128)S(1)}, f32[256,1024]{1,0:T(8,128)}, u32[]{:S(2)}) copy-start(f32[256,1024]{1,0:T(8,128)} %get-tuple-element.15) | copy-start | bytes 3145732
  134.2 1.4 %copy-start.1 = (f32[256,512]{1,0:T(8,128)S(1)}, f32[256,512]{1,0:T(8,128)}, u32[]{:S(2)}) copy-start(f32[256,512]{1,0:T(8,128)} %get-tuple-element.16) | copy-start | bytes 1572868
